TPU v7x, 128 devices: a whole 4x4x4 slice. The times are simulated.
128 devices in a mesh: dp: 2 (over y_lo), pipe: 16 (over y_hi, z, core), tensor: 4 (over x).
Axes of the slice: x: 4, y: 4 (y_hi: 2, y_lo: 2; y = y_hi * 2 + y_lo), z: 4, core: 2. Of those that a mesh axis runs over, the one named last changes fastest.
Arguments:
- tokens: int32 [256], P('dp'), may hold values from 0 to 25135
- targets: int32 [256], P('dp'), may hold values from 0 to 25135
- hidden: bfloat16 [256, 12288], P('dp', 'pipe'), may hold values from -12 to 12
- embed_grad: bfloat16 [256, 12288], P('dp', 'pipe'), may hold values from -6 to 6
- word_matrix: bfloat16 [25136, 12288], P('tensor', 'pipe'), may hold values from -1 to 1
Outputs:
- token_loss: float32 [256], P(('dp', 'pipe'))
- hidden_grad: bfloat16 [256, 12288], P(('dp', 'tensor'), 'pipe')
- word_grad: float32 [25136, 12288], P(('tensor', 'dp'), 'pipe')
All inputs are finite; a program needn't handle non-finite values.
Results may differ from a plain program's by a relative error of at most 0.0034.
Values may be sent and summed in bfloat16 or wider, within the bound.
A program may use at most 128 MiB of HBM per device.

v0:
```python
import jax
import jax.numpy as jnp
from jax import lax
from jax.sharding import PartitionSpec as P


def softmax_grad(logits, target_rows, offset):
    columns = lax.broadcasted_iota(jnp.int32, logits.shape, 1)
    chosen = columns == (target_rows - offset)[:, None]
    picked = jnp.sum(jnp.where(chosen, logits, 0.0), axis=1)
    local_max = jnp.max(logits, axis=1)
    row_max = lax.pmax(local_max, "tensor")
    shifted = jnp.exp(logits - row_max[:, None])
    row_total, target_logit = lax.psum((jnp.sum(shifted, axis=1), picked), "tensor")
    softmax = shifted / row_total[:, None]
    logit_grad = (softmax - chosen.astype(jnp.float32)).astype(jnp.bfloat16)
    token_loss = jnp.log(row_total) + row_max - target_logit
    return (logit_grad, token_loss)


def word_terms(grad_cols, hidden_rows_all, embed_rows, token_ids, first_vocab):
    contract_first = (((0,), (0,)), ((), ()))
    num_rows = grad_cols.shape[1]
    head_part = lax.dot_general(
        grad_cols, hidden_rows_all, contract_first, preferred_element_type=jnp.float32
    )
    vocab_ids = first_vocab + lax.broadcasted_iota(jnp.int32, (1, num_rows), 1)
    one_hot = (token_ids[:, None] == vocab_ids).astype(jnp.bfloat16)
    lookup = lax.dot_general(
        one_hot, embed_rows, contract_first, preferred_element_type=jnp.float32
    )
    return head_part + lookup


def local(tokens, targets, hidden, embed_grad, word_matrix):
    tok_count = hidden.shape[0]
    vocab_rows = word_matrix.shape[0]
    sections = lax.axis_size("pipe")
    row_share = tok_count // sections
    offset = lax.axis_index("tensor") * vocab_rows
    first_row = lax.axis_index("pipe") * row_share
    contract_last = (((1,), (1,)), ((), ()))
    partial_logits = lax.dot_general(
        hidden, word_matrix, contract_last, preferred_element_type=jnp.float32
    )
    logits = lax.psum(partial_logits, "pipe")
    logit_grad, every_loss = softmax_grad(logits, targets, offset)
    token_loss = lax.dynamic_slice_in_dim(every_loss, first_row, row_share, 0)
    hidden_grad = lax.psum_scatter(
        jnp.dot(logit_grad, word_matrix, preferred_element_type=jnp.float32),
        "tensor",
        scatter_dimension=0,
        tiled=True,
    ).astype(jnp.bfloat16)
    word_grad = lax.psum_scatter(
        word_terms(logit_grad, hidden, embed_grad, tokens, offset),
        "dp",
        scatter_dimension=0,
        tiled=True,
    )
    return (token_loss, hidden_grad, word_grad)


def solution(mesh):
    return jax.shard_map(
        local,
        mesh=mesh,
        in_specs=(P("dp"), P("dp"), P("dp", "pipe"), P("dp", "pipe"), P("tensor", "pipe")),
        out_specs=(P(("dp", "pipe")), P(("dp", "tensor"), "pipe"), P(("tensor", "dp"), "pipe")),
        check_vma=False,
    )
```

profile of v0, /device:TPU:1, one launch (start us, length us, event | category | flops | bytes accessed | tf_op | source)
XLA Modules:
  0.0 478.2 jit_solution(12738494134516305739)
XLA Ops:
  7.2 0.0 copy-start
  7.2 0.0 all-reduce.5.cloned.1.call-start
  7.2 0.9 copy-done
  8.1 8.1 %fusion.7 = f32[128,6284]{0,1:T(8,128)} fusion(bf16[128,768]{1,0:T(8,128)(2,1)S(1)} %copy-done, bf16[6284,768]{1,0:T(8,128)(2,1)} %param.9), kind=kOutput, calls=%fused_computation.15 | convolution fusion | flops 1235484672 | bytes 13066240 | tf_op jit(solution)/shard_map/dot_general | solution.py:43
  16.2 0.0 copy-start.5
  16.2 0.0 copy-start.6
  16.2 0.0 all-reduce.5.cloned.1.call-update
  16.2 0.0 reduce-scatter.4.cloned.1.call-start
  16.3 0.6 copy-done.5
  16.9 0.6 dynamic-slice.4
  18.1 0.0 copy-done.6
  18.1 148.9 %all-reduce.5.cloned.1.call-done = f32[128,6284]{0,1:T(8,128)} async-done(((f32[128,6284]{0,1:T(8,128)}), f32[128,6284]{0,1:T(8,128)}) %all-reduce.5.cloned.1.call-update) | async-done | bytes 3217424 | tf_op jit(solution)/shard_map/psum | solution.py:46
  167.1 0.0 copy-start.2
  167.1 2.9 reduce_max.9
  170.0 8.4 %pmax.7 = f32[128]{0:T(128)S(1)} all-reduce(f32[128]{0:T(128)S(1)} %reduce_max.9), channel_id=1, replica_groups=mesh['dp'=2,'pipe'=16,'tensor'=4] {'tensor'}, use_global_device_ids=true, to_apply=%region_2.3 | all-reduce | flops 128 | bytes 1024 | tf_op jit(solution)/shard_map/pmax | solution.py:12
  178.4 0.0 copy-done.2
  178.4 0.9 fusion.2
  179.2 6.0 %all-reduce.2 = (f32[128]{0:T(128)S(1)}, f32[128]{0:T(128)S(1)}) all-reduce(f32[128]{0:T(128)S(1)} %get-tuple-element.4, f32[128]{0:T(128)S(1)} %get-tuple-element.3), channel_id=1, replica_groups=mesh['dp'=2,'pipe'=16,'tensor'=4] {'tensor'}, use_global_device_ids=true, to_apply=%region_6.7 | all-reduce | flops 256 | bytes 2048 | tf_op jit(solution)/shard_map/psum | solution.py:14
  185.2 6.4 %fusion.6 = f32[128,768]{1,0:T(8,128)} fusion(bf16[6284,768]{1,0:T(8,128)(2,1)} %param.9, f32[128,6284]{0,1:T(8,128)S(1)} %copy-done.2, f32[128]{0:T(128)S(1)} %get-tuple-element.6, s32[128]{0:T(128)S(1)} %broadcast_subtract_fusion, f32[128]{0:T(128)S(1)} %pmax.7), kind=kOutput, calls=%fused_computation.14 | convolution fusion | flops 1240310784 | bytes 13264384 | tf_op jit(solution)/shard_map/dot_general | solution.py:50
  191.6 0.0 reduce-scatter.4.cloned.1.call-update
  191.6 0.0 copy-start.3
  191.6 0.0 copy-start.4
  191.7 8.0 %fusion.5 = f32[6284,768]{1,0:T(8,128)} fusion(bf16[128,768]{1,0:T(8,128)(2,1)S(1)} %copy-done, f32[128,6284]{0,1:T(8,128)S(1)} %copy-done.2, f32[128]{0:T(128)S(1)} %get-tuple-element.6, s32[128]{0:T(128)S(1)} %broadcast_subtract_fusion, f32[128]{0:T(128)S(1)} %pmax.7), kind=kOutput, calls=%fused_computation.13 | convolution fusion | flops 1240310784 | bytes 22720000 | tf_op jit(solution)/shard_map/dot_general | solution.py:24
  199.7 0.0 copy-done.3
  199.7 0.0 copy-done.4
  199.7 15.9 %convolution_add_fusion = f32[6284,768]{1,0:T(8,128)} fusion(f32[6284,768]{1,0:T(8,128)} %fusion.5, bf16[128,768]{1,0:T(8,128)(2,1)S(1)} %copy-done.3, s32[6284]{0:T(1024)S(1)} %iota_add_fusion, s32[128]{0:T(128)S(1)} %copy-done.4), kind=kOutput, calls=%fused_computation | convolution fusion | flops 1241115136 | bytes 38831152 | tf_op jit(solution)/shard_map/dot_general | solution.py:29
  215.6 216.3 %fusion = f32[3144,768]{1,0:T(8,128)} fusion(f32[6284,768]{1,0:T(8,128)} %convolution_add_fusion), kind=kCustom, calls=%all-reduce-scatter | all-reduce-scatter fusion | flops 4829185 | bytes 28963328
  432.0 0.7 slice
  432.7 3.6 collective-permute-start
  436.3 0.6 dynamic_slice.3
  436.9 0.2 collective-permute-done
  437.0 24.5 %concatenate = f32[3146,768]{1,0:T(8,128)} concatenate(f32[2,768]{1,0:T(2,128)S(1)} %collective-permute-done, f32[3144,768]{1,0:T(8,128)} %fusion), dimensions={0} | concatenate | bytes 19329024
  461.5 0.0 copy-start.1
  461.5 8.4 %constant_dynamic-slice_fusion = f32[3142,768]{1,0:T(8,128)} fusion(f32[3146,768]{1,0:T(8,128)} %concatenate, u32[]{:S(6)} %subtract), kind=kLoop, calls=%fused_computation.10 | loop fusion | bytes 19304452
  469.9 0.0 reduce-scatter.4.cloned.1.call-done
  469.9 1.5 convert_element_type.12
  471.4 0.0 copy-done.1
  (3 shorter events, 0.0 us)
Async XLA Ops:
  7.2 0.9 copy-start
  7.2 159.9 %all-reduce.5.cloned.1.call-start = ((), (), s32[]{:S(2)}) async-start(), calls=%async_computation.1 | async-start | bytes 6438912 | tf_op jit(solution)/shard_map/psum | solution.py:46
  16.2 0.7 copy-start.5
  16.2 1.9 copy-start.6
  16.2 453.6 %reduce-scatter.4.cloned.1.call-start = ((), (), s32[]{:S(2)}) async-start(), calls=%async_computation.2 | async-start | bytes 491520 | tf_op jit(solution)/shard_map/reduce_scatter | solution.py:49
  167.1 11.3 %copy-start.2 = (f32[128,6284]{0,1:T(8,128)S(1)}, f32[128,6284]{0,1:T(8,128)}, u32[]{:S(2)}) copy-start(f32[128,6284]{0,1:T(8,128)} %all-reduce.5.cloned.1.call-done) | copy-start | bytes 9652228
  191.6 8.1 %copy-start.3 = (bf16[128,768]{1,0:T(8,128)(2,1)S(1)}, bf16[128,768]{1,0:T(8,128)(2,1)}, u32[]{:S(2)}) copy-start(bf16[128,768]{1,0:T(8,128)(2,1)} %param.8) | copy-start | bytes 589828
  191.6 8.1 %copy-start.4 = (s32[128]{0:T(128)S(1)}, s32[128]{0:T(128)}, u32[]{:S(2)}) copy-start(s32[128]{0:T(128)} %param.5) | copy-start | bytes 1540
  432.7 4.3 collective-permute-start
  461.5 9.9 %copy-start.1 = (bf16[128,768]{1,0:T(8,128)(2,1)S(1)}, bf16[128,768]{1,0:T(8,128)(2,1)}, u32[]{:S(2)}) copy-start(bf16[128,768]{1,0:T(8,128)(2,1)} %param.7) | copy-start | bytes 589828
Sparse Core Ops, SparseCore 0:
  16.4 150.6 all-reduce.4
  191.8 19.7 reduce-scatter.3
where the time goes:
time: 485 us; the launch traced here: 478 us
  blocking collectives  231 us (48%)
  waiting for transfers between devices  149 us (31%)
  matrix products  38.5 us (8%)
  local copies, waits for them, and re-layouts  36.2 us (7%)
  between operations  14.8 us (3%)
  other arithmetic  5.29 us (1%)
    unnamed x1, blocking collectives  216 us
    psum x1, waiting for transfers between devices, local(): logits = lax.psum(partial_logits, 'pipe')  149 us
    unnamed x18, local copies, waits for them, and re-layouts  35.6 us
    dot_general x1, matrix products, word_terms(): lax.dot_general(one_hot, embed_rows, contract_first, preferred_element_ty...  15.9 us
  transfers between devices with their start and end apart: 3, of which 2 were waited for; matrix products, arithmetic and copies ran while one was open for 58% of the time, Pallas kernels for 0%

commit v1 on v0

v1 whole, which is shorter than its diff:
```python
import functools

import jax
import jax.numpy as jnp
from jax import lax
from jax.experimental import pallas as pl
from jax.experimental.pallas import tpu as pltpu
from jax.sharding import PartitionSpec as P

MESH = pl.DeviceIdType.MESH
BF16, F32, I32, I16 = jnp.bfloat16, jnp.float32, jnp.int32, jnp.int16

DM = 768
VS = 6284
VH = 3142
SH = 6
MAIN = 3136
NC = 3200
CH = 640
NJ = NC // CH
SR = 320
NS = 2 * NJ
TOP = 32767.0


class Place:
    def __init__(self):
        self.d = lax.axis_index("dp")
        self.p = lax.axis_index("pipe")
        self.t = lax.axis_index("tensor")
        self.c = self.p % 2
        self.k = self.p // 2
        self.y = self.k // 4
        self.z = self.k % 4

    def chip(self, k):
        return {"pipe": k * 2 + self.c}

    def partner(self):
        return {"pipe": self.k * 2 + (1 - self.c)}

    def group(self, g):
        return {"dp": g // 4, "tensor": g % 4}


def token_block(k, c):
    y, z = k // 4, k % 4
    return (z % 2) * 8 + (y * 2 + z // 2) * 2 + c


def quantize(x):
    top = jnp.maximum(jnp.max(jnp.abs(x), axis=-1, keepdims=True), 1e-30)
    return jnp.round(x * (TOP / top)).astype(I32).astype(I16), top


def comm_kernel(
    tok_ref, tgt_ref, hid_hbm, emb_hbm, w_hbm, tail0_ref, tail1_ref,
    g_out, hid_out, emb_out, tok_out, loss_out, hg_out,
    wwin, wsh, hid, part, xch, qbuf, scl, rs, rs_scl, tokx, tgtx, lbuf, stat, gbuf,
    hgf, hq, hs, hr, hr_scl,
    w_sem, hid_sem, px_send, px_recv, xc_send, xc_recv, rs_send, rs_recv, sc_send, sc_recv,
    st_send, st_recv, ag_send, ag_recv, pf_send, pf_recv, hg_send, hg_recv, hs_send, hs_recv,
    out_sem,
):
    me = Place()
    d, c, k = me.d, me.c, me.k
    g_me = d * 4 + me.t

    def remote(src, dst, ssem, rsem, to):
        return pltpu.make_async_remote_copy(
            src_ref=src, dst_ref=dst, send_sem=ssem, recv_sem=rsem, device_id=to, device_id_type=MESH
        )

    def w_copy(j):
        rows = CH if j < NJ - 1 else MAIN - (NJ - 1) * CH
        start = pl.multiple_of(d * MAIN + j * CH, 16)
        return pltpu.make_async_copy(
            w_hbm.at[pl.ds(start, rows)], wwin.at[pl.ds(j * CH, rows)], w_sem.at[j]
        )

    own_hid = pltpu.make_async_copy(hid_hbm, hid.at[d], hid_sem)
    own_hid.start()
    for j in range(NJ):
        w_copy(j).start()
    own_emb = pltpu.make_async_copy(emb_hbm, emb_out.at[d], out_sem.at[0])
    own_emb.start()

    bar = pltpu.get_barrier_semaphore()
    pl.semaphore_signal(bar, inc=1, device_id=me.partner(), device_id_type=MESH)
    for o in range(1, 8):
        pl.semaphore_signal(bar, inc=1, device_id=me.chip((k + o) % 8), device_id_type=MESH)
        pl.semaphore_signal(bar, inc=1, device_id=me.group((g_me + o) % 8), device_id_type=MESH)
    pl.semaphore_wait(bar, 15)

    other = {"dp": 1 - d}
    give_hid = remote(hid_hbm, hid.at[d], px_send.at[0], px_recv.at[0], other)
    give_hid.start()
    give_tgt = remote(tgt_ref, tgtx, px_send.at[1], px_recv.at[1], other)
    give_tgt.start()
    give_tok = remote(tok_ref, tokx, px_send.at[2], px_recv.at[2], other)
    give_tok.start()

    row16 = lax.broadcasted_iota(I32, (16, DM), 0)
    tail0 = tail0_ref[...].astype(F32)
    tail1 = jnp.where(row16 < VS - 2 * MAIN, tail1_ref[...].astype(F32), 0.0)
    wwin[pl.ds(MAIN, 16), :] = jnp.where(d == 0, tail0, tail1).astype(BF16)
    wwin[pl.ds(MAIN + 16, NC - MAIN), :] = jnp.zeros((NC - MAIN, DM), BF16)
    scl[...] = jnp.zeros_like(scl)

    def xc_copy(s):
        return remote(part.at[s, :, 1 - c], xch.at[s], xc_send.at[s], xc_recv.at[s], me.partner())

    def target_chip(i, s):
        ph = jnp.where(s < NJ, d, 1 - d)
        return (i // 2) * 4 + 2 * (i % 2) + ph

    def rs_copy(i, s):
        return remote(
            qbuf.at[s, i], rs.at[k, s % NJ], rs_send.at[s, i], rs_recv.at[k, s % NJ],
            me.chip(target_chip(i, s)),
        )

    def sc_copy(i, h):
        return remote(
            scl.at[h, i], rs_scl.at[k], sc_send.at[h, i], sc_recv.at[k], me.chip(target_chip(i, h * NJ))
        )

    def multiply(s):
        j = s % NJ
        who = jnp.where(s < NJ, d, 1 - d)
        cols = pl.ds(pl.multiple_of(j * CH, CH), CH)
        prod = lax.dot_general(
            hid[who], wwin[cols, :], (((1,), (1,)), ((), ())), preferred_element_type=F32
        )
        part[s] = prod.reshape(4, 2, 16, CH)
        xc_copy(s).start()

    def finish(s):
        j = s % NJ
        h = s // NJ
        xc_copy(s).wait_recv()
        total = part[s, :, c] + xch[s]
        code, top = quantize(total)
        qbuf[s] = code
        lane = lax.broadcasted_iota(I32, (4, 16, 128), 2)
        scl[h] = jnp.where(lane == j, top, scl[h])
        for i in range(4):
            to = target_chip(i, s)

            @pl.when(to != k)
            def _():
                rs_copy(i, s).start()

            @pl.when(to == k)
            def _():
                rs[k, j] = qbuf[s, i]

            @pl.when(jnp.logical_and(to != k, j == NJ - 1))
            def _():
                sc_copy(i, h).start()

            @pl.when(jnp.logical_and(to == k, j == NJ - 1))
            def _():
                rs_scl[k] = scl[h, i]

    own_hid.wait()

    def step(s, carry):
        for j in range(NJ):

            @pl.when(s == j)
            def _():
                w_copy(j).wait()

        @pl.when(s == NJ)
        def _():
            give_hid.wait_recv()

        multiply(s)

        @pl.when(s > 0)
        def _():
            finish(s - 1)

        return carry

    lax.fori_loop(0, NS, step, 0)
    finish(NS - 1)

    give_emb = remote(emb_hbm, emb_out.at[d], px_send.at[3], px_recv.at[3], other)
    give_emb.start()
    hid_copy = pltpu.make_async_copy(hid, hid_out, out_sem.at[1])
    hid_copy.start()

    def shift(i, carry):
        rows = pl.multiple_of(i * SR, 64)
        wide = wwin[pl.ds(rows, SR + 16), :].astype(F32)
        moved = jnp.where(d == 0, wide[0:SR, :], wide[SH : SH + SR, :])
        wsh[pl.ds(rows, SR), :] = moved.astype(BF16)
        return carry

    lax.fori_loop(0, NC // SR, shift, 0)
    row_l = lax.broadcasted_iota(I32, (NC - MAIN, DM), 0) + MAIN
    end = wsh[pl.ds(MAIN, NC - MAIN), :].astype(F32)
    wsh[pl.ds(MAIN, NC - MAIN), :] = jnp.where(row_l < VH, end, 0.0).astype(BF16)

    give_tgt.wait_recv()
    give_tok.wait_recv()
    block = token_block(k, c)
    mine = (block // 8) == d
    tgt_row = jnp.where(mine, tgt_ref[...], tgtx[...]).astype(F32)
    lane16 = lax.broadcasted_iota(I32, (16, 128), 1)
    sub16 = lax.broadcasted_iota(I32, (16, 128), 0)
    tgt = jnp.sum(
        jnp.where(lane16 == sub16 + (block % 8) * 16, tgt_row, 0.0), axis=1, keepdims=True
    ).astype(I32)
    offset = me.t * VS + d * VH
    tok_d, tok_o = tok_ref[...], tokx[...]
    sub8 = lax.broadcasted_iota(I32, (8, 128), 0)
    tok_out[...] = jnp.where(sub8 == d, tok_d, tok_o)

    for q in range(8):

        @pl.when(q != k)
        def _():
            for j in range(NJ):
                remote(
                    qbuf.at[0, 0], rs.at[q, j], rs_send.at[0, 0], rs_recv.at[q, j], me.chip(q)
                ).wait_recv()
            remote(
                scl.at[0, 0], rs_scl.at[q], sc_send.at[0, 0], sc_recv.at[q], me.chip(q)
            ).wait_recv()

    for j in range(NJ):
        total = jnp.zeros((16, CH), F32)
        for q in range(8):
            unit = rs_scl[q][:, j : j + 1] * (1.0 / TOP)
            total += rs[q, j].astype(I32).astype(F32) * unit
        lbuf[:, j * CH : (j + 1) * CH] = total

    logits = pltpu.roll(lbuf[...], (NC - SH * d) % NC, 1)
    col = lax.broadcasted_iota(I32, (16, NC), 1)
    valid = col < VH
    logits = jnp.where(valid, logits, -1e30)
    chosen = col == (tgt - offset)
    chosen = jnp.logical_and(chosen, valid)
    m_loc = jnp.max(logits, axis=1, keepdims=True)
    e = jnp.where(valid, jnp.exp(logits - m_loc), 0.0)
    s_loc = jnp.sum(e, axis=1, keepdims=True)
    t_loc = jnp.sum(jnp.where(chosen, logits, 0.0), axis=1, keepdims=True)
    stat[g_me] = jnp.where(lane16 == 0, m_loc, jnp.where(lane16 == 1, s_loc, t_loc))

    def st_copy(o):
        return remote(
            stat.at[g_me], stat.at[g_me], st_send.at[o], st_recv.at[g_me], me.group((g_me + o) % 8)
        )

    for o in range(1, 8):
        st_copy(o).start()
    for o in range(1, 8):
        q = (g_me + o) % 8
        remote(stat.at[g_me], stat.at[q], st_send.at[o], st_recv.at[q], me.group(q)).wait_recv()
    row_max = stat[0][:, 0:1]
    for q in range(1, 8):
        row_max = jnp.maximum(row_max, stat[q][:, 0:1])
    row_total = jnp.zeros((16, 1), F32)
    target_logit = jnp.zeros((16, 1), F32)
    for q in range(8):
        row_total += stat[q][:, 1:2] * jnp.exp(stat[q][:, 0:1] - row_max)
        target_logit += stat[q][:, 2:3]
    loss = jnp.log(row_total) + row_max - target_logit
    grad = e * (jnp.exp(m_loc - row_max) / row_total) - jnp.where(chosen, 1.0, 0.0)
    hi = loss.astype(BF16).astype(F32)
    mid = (loss - hi).astype(BF16).astype(F32)
    low = loss - hi - mid
    grad = jnp.where(col == VH, hi, grad)
    grad = jnp.where(col == VH + 1, mid, grad)
    grad = jnp.where(col == VH + 2, low, grad)

    def rows_of(b):
        return pl.ds(pl.multiple_of(b * 16, 16), 16)

    gbuf[rows_of(block), :] = grad.astype(BF16)

    def ag_copy(o, source):
        rows = rows_of(token_block(source, c))
        return remote(
            gbuf.at[rows], gbuf.at[rows], ag_send.at[o], ag_recv.at[source], me.chip((k + o) % 8)
        )

    def pf_copy(source, core):
        rows = rows_of(token_block(source, core))
        return remote(
            gbuf.at[rows], gbuf.at[rows], pf_send.at[source], pf_recv.at[source], me.partner()
        )

    for o in range(1, 8):
        ag_copy(o, k).start()
    pf_copy(k, c).start()
    for o in range(1, 8):
        source = (k + o) % 8
        ag_copy(o, source).wait_recv()
        pf_copy(source, c).start()
    for q in range(8):
        pf_copy(q, 1 - c).wait_recv()

    g_copy = pltpu.make_async_copy(gbuf, g_out, out_sem.at[2])
    g_copy.start()

    def columns(n, carry):
        cols = pl.ds(pl.multiple_of(n * 256, 256), 256)
        hgf[:, cols] = jnp.dot(gbuf[...], wsh[:, cols], preferred_element_type=F32)
        return carry

    lax.fori_loop(0, DM // 256, columns, 0)
    for g in range(8):
        code, top = quantize(hgf[pl.ds(g * 32, 32), :])
        hq[g] = code
        hs[g] = jnp.broadcast_to(top, (32, 128))

    def hg_copy(o):
        q = (g_me + o) % 8
        return remote(hq.at[q], hr.at[g_me], hg_send.at[o], hg_recv.at[g_me], me.group(q))

    def hs_copy(o):
        q = (g_me + o) % 8
        return remote(hs.at[q], hr_scl.at[g_me], hs_send.at[o], hs_recv.at[g_me], me.group(q))

    for o in range(1, 8):
        hg_copy(o).start()
        hs_copy(o).start()
    hr[g_me] = hq[g_me]
    hr_scl[g_me] = hs[g_me]

    tile = gbuf[rows_of(d * 8 + me.p // 2), pl.ds(NC - 128, 128)].astype(F32)
    half = jnp.where(me.p % 2 == 0, tile[0:8, :], tile[8:16, :])
    lane8 = lax.broadcasted_iota(I32, (8, 128), 1) + (NC - 128)
    here = jnp.logical_and(lane8 >= VH, lane8 < VH + 3)
    value = jnp.sum(jnp.where(here, half, 0.0), axis=1, keepdims=True)
    loss_out[...] = jnp.broadcast_to(value, (8, 128))

    for o in range(1, 8):
        q = (g_me + o) % 8
        remote(hq.at[q], hr.at[q], hg_send.at[o], hg_recv.at[q], me.group(q)).wait_recv()
        remote(hs.at[q], hr_scl.at[q], hs_send.at[o], hs_recv.at[q], me.group(q)).wait_recv()
    total = jnp.zeros((32, DM), F32)
    for q in range(8):
        total += hr[q].astype(I32).astype(F32) * (hr_scl[q][:, 0:1] * (1.0 / TOP))
    hg_out[...] = total.astype(BF16)

    give_hid.wait_send()
    give_tgt.wait_send()
    give_tok.wait_send()
    give_emb.wait()
    own_emb.wait()
    hid_copy.wait()
    g_copy.wait()

    def drain(s, carry):
        xc_copy(s).wait_send()
        for i in range(4):

            @pl.when(target_chip(i, s) != k)
            def _():
                rs_copy(i, s).wait_send()

        return carry

    lax.fori_loop(0, NS, drain, 0)
    for h in range(2):
        for i in range(4):

            @pl.when(target_chip(i, h * NJ) != k)
            def _():
                sc_copy(i, h).wait_send()

    for o in range(1, 8):
        st_copy(o).wait_send()
        ag_copy(o, k).wait_send()
        hg_copy(o).wait_send()
        hs_copy(o).wait_send()
    for q in range(8):
        pf_copy(q, c).wait_send()


def comm_call(tokens, targets, hidden, embed, word):
    any_, vmem = pl.BlockSpec(memory_space=pl.ANY), pl.BlockSpec(memory_space=pltpu.VMEM)
    dma = pltpu.SemaphoreType.DMA
    rows_block = MAIN // 16
    return pl.pallas_call(
        comm_kernel,
        grid=(1,),
        out_shape=(
            jax.ShapeDtypeStruct((256, NC), BF16),
            jax.ShapeDtypeStruct((2, 128, DM), BF16),
            jax.ShapeDtypeStruct((2, 128, DM), BF16),
            jax.ShapeDtypeStruct((8, 128), I32),
            jax.ShapeDtypeStruct((8, 128), F32),
            jax.ShapeDtypeStruct((32, DM), BF16),
        ),
        in_specs=[
            vmem, vmem, any_, any_, any_,
            pl.BlockSpec((16, DM), lambda i: (rows_block, 0)),
            pl.BlockSpec((16, DM), lambda i: (2 * rows_block, 0)),
        ],
        out_specs=(any_, any_, any_, vmem, vmem, vmem),
        scratch_shapes=[
            pltpu.VMEM((NC + 16, DM), BF16),
            pltpu.VMEM((NC, DM), BF16),
            pltpu.VMEM((2, 128, DM), BF16),
            pltpu.VMEM((NS, 4, 2, 16, CH), F32),
            pltpu.VMEM((NS, 4, 16, CH), F32),
            pltpu.VMEM((NS, 4, 16, CH), I16),
            pltpu.VMEM((2, 4, 16, 128), F32),
            pltpu.VMEM((8, NJ, 16, CH), I16),
            pltpu.VMEM((8, 16, 128), F32),
            pltpu.VMEM((1, 128), I32),
            pltpu.VMEM((1, 128), I32),
            pltpu.VMEM((16, NC), F32),
            pltpu.VMEM((8, 16, 128), F32),
            pltpu.VMEM((256, NC), BF16),
            pltpu.VMEM((256, DM), F32),
            pltpu.VMEM((8, 32, DM), I16),
            pltpu.VMEM((8, 32, 128), F32),
            pltpu.VMEM((8, 32, DM), I16),
            pltpu.VMEM((8, 32, 128), F32),
            dma((NJ,)),
            dma,
            dma((4,)),
            dma((4,)),
            dma((NS,)),
            dma((NS,)),
            dma((NS, 4)),
            dma((8, NJ)),
            dma((2, 4)),
            dma((8,)),
            dma((8,)),
            dma((8,)),
            dma((8,)),
            dma((8,)),
            dma((8,)),
            dma((8,)),
            dma((8,)),
            dma((8,)),
            dma((8,)),
            dma((8,)),
            dma((3,)),
        ],
        compiler_params=pltpu.CompilerParams(
            collective_id=0, has_side_effects=True, vmem_limit_bytes=48 * 2**20
        ),
        name="logit_grad",
    )(tokens, targets, hidden, embed, word, word, word)


RB = 640


def word_kernel(g_ref, hid_ref, emb_ref, tok_ref, loss_ref, hg_ref, out_ref, loss_out, hg_out):
    i = pl.program_id(0)
    base = lax.axis_index("tensor") * VS + lax.axis_index("dp") * VH + i * RB
    rows = lax.broadcasted_iota(I32, (RB, 128), 0) + base
    tok = tok_ref[...]
    hot = jnp.concatenate(
        [jnp.where(rows == tok[h : h + 1, :], 1.0, 0.0).astype(BF16) for h in range(2)], axis=1
    )
    head = lax.dot_general(
        g_ref[...], hid_ref[...], (((0,), (0,)), ((), ())), preferred_element_type=F32
    )
    out_ref[...] = head + jnp.dot(hot, emb_ref[...], preferred_element_type=F32)

    @pl.when(i == 0)
    def _():
        sub = lax.broadcasted_iota(I32, (8, 128), 0)
        lane = lax.broadcasted_iota(I32, (8, 128), 1)
        row = jnp.sum(jnp.where(sub == lane, loss_ref[...], 0.0), axis=0, keepdims=True)
        loss_out[...] = row[:, 0:8]
        hg_out[...] = hg_ref[...]


def word_call(grad, hid, emb, tok, loss, hg):
    def whole(*shape):
        return pl.BlockSpec(shape, lambda i: (0,) * len(shape))

    return pl.pallas_call(
        word_kernel,
        grid=(pl.cdiv(VH, RB),),
        out_shape=(
            jax.ShapeDtypeStruct((VH, DM), F32),
            jax.ShapeDtypeStruct((1, 8), F32),
            jax.ShapeDtypeStruct((32, DM), BF16),
        ),
        in_specs=[
            pl.BlockSpec((256, RB), lambda i: (0, i)),
            whole(256, DM), whole(256, DM), whole(8, 128), whole(8, 128), whole(32, DM),
        ],
        out_specs=(pl.BlockSpec((RB, DM), lambda i: (i, 0)), whole(1, 8), whole(32, DM)),
        compiler_params=pltpu.CompilerParams(vmem_limit_bytes=48 * 2**20),
        name="word_grad",
    )(grad, hid, emb, tok, loss, hg)


def local(tokens, targets, hidden, embed_grad, word_matrix):
    grad, hid, emb, tok, loss, hg = comm_call(
        tokens.reshape(1, 128), targets.reshape(1, 128), hidden, embed_grad, word_matrix
    )
    word, loss, hg = word_call(
        grad, hid.reshape(256, DM), emb.reshape(256, DM), tok, loss, hg
    )
    return loss.reshape(8), hg, word


def solution(mesh):
    return jax.shard_map(
        local,
        mesh=mesh,
        in_specs=(P("dp"), P("dp"), P("dp", "pipe"), P("dp", "pipe"), P("tensor", "pipe")),
        out_specs=(P(("dp", "pipe")), P(("dp", "tensor"), "pipe"), P(("tensor", "dp"), "pipe")),
        check_vma=False,
    )
```

time: 485 us -> 69.3 us (0.14); the launches traced: 478 us -> 69.1 us
  blocking collectives: 231 us -> 0 us
  waiting for transfers between devices: 149 us -> 0 us
  Pallas kernels: 0 us -> 65.3 us
  matrix products: 38.5 us -> 0 us
  local copies, waits for them, and re-layouts: 36.2 us -> 3.16 us
  between operations: 14.8 us -> 0.65 us
  other arithmetic: 5.29 us -> 0 us
    unnamed x1 -> x0, blocking collectives: 216 us -> none
    psum x1 -> x0, waiting for transfers between devices: 149 us -> none  [local(): logits = lax.psum(partial_logits, 'pipe')]
    pallas_call x0 -> x2, Pallas kernels: none -> 65.3 us  [the longest x1 59.4 us: comm_call(): pl.pallas_call(comm_kernel, grid=(1,), out_shape=(jax.ShapeDtypeStruct((2...]
    dot_general x4 -> x0, matrix products: 38.5 us -> none  [the longest x1 15.9 us: word_terms(): lax.dot_general(one_hot, embed_rows, contract_first, preferred_element_ty...]
    unnamed x18 -> x8, local copies, waits for them, and re-layouts: 35.6 us -> 3.16 us
    pmax x1 -> x0, blocking collectives: 8.4 us -> none  [softmax_grad(): row_max = lax.pmax(local_max, 'tensor')]
    psum x1 -> x0, blocking collectives: 6 us -> none  [softmax_grad(): lax.psum((jnp.sum(shifted, axis=1), picked), 'tensor')]
  transfers between devices with their start and end apart: 3 -> 0, of which waited for: 2 -> 0; matrix products, arithmetic and copies ran while one was open for 58% -> 0% of each run, Pallas kernels for 0% -> 0%
where the time goes in v1:
time: 69.3 us; the launch traced here: 69.1 us
  Pallas kernels  65.3 us (94%)
  local copies, waits for them, and re-layouts  3.16 us (5%)
    pallas_call x1, Pallas kernels, comm_call(): pl.pallas_call(comm_kernel, grid=(1,), out_shape=(jax.ShapeDtypeStruct((2...  59.4 us
    pallas_call x1, Pallas kernels, word_call(): pl.pallas_call(word_kernel, grid=(pl.cdiv(VH, RB),), out_shape=(jax.Shape...  5.95 us
    unnamed x8, local copies, waits for them, and re-layouts  3.16 us

profile of v1, /device:TPU:1, one launch (start us, length us, event | category | flops | bytes accessed | tf_op | source)
XLA Modules:
  0.0 69.1 jit_solution(5509676138652596867)
XLA Ops:
  0.6 0.0 copy-start
  0.6 0.9 %copy-done = bf16[128,768]{1,0:T(8,128)(2,1)S(1)} copy-done((bf16[128,768]{1,0:T(8,128)(2,1)S(1)}, bf16[128,768]{1,0:T(8,128)(2,1)}, u32[]{:S(2)}) %copy-start) | copy-done | bytes 196632
  1.6 0.0 copy-start.1
  1.6 0.9 %copy-done.1 = bf16[128,768]{1,0:T(8,128)(2,1)S(1)} copy-done((bf16[128,768]{1,0:T(8,128)(2,1)S(1)}, bf16[128,768]{1,0:T(8,128)(2,1)}, u32[]{:S(2)}) %copy-start.1) | copy-done | bytes 196632
  2.5 0.0 copy-start.2
  2.5 0.7 copy-done.2
  3.1 0.0 copy-start.3
  3.1 0.7 copy-done.3
  3.8 59.4 %logit_grad.1 = (bf16[256,3200]{1,0:T(8,128)(2,1)S(1)}, bf16[2,128,768]{2,1,0:T(8,128)(2,1)S(1)}, bf16[2,128,768]{2,1,0:T(8,128)(2,1)S(1)}, s32[8,128]{1,0:T(8,1...) custom-call(s32[1,128]{1,0:T(1,128)S(1)} %bitcast.7, s32[1,128]{1,0:T(1,128)S(1)} %bitcast.8, ...), custom_call_target="tpu_custom_call" | custom-call | tf_op jit(solution)/shard_map/logit_grad/pallas_call | solution.py:390
  63.2 5.9 %word_grad.1 = (f32[3142,768]{1,0:T(8,128)}, f32[1,8]{1,0:T(1,128)}, bf16[32,768]{1,0:T(8,128)(2,1)}) custom-call(bf16[256,3200]{1,0:T(8,128)(2,1)S(1)} %get-tuple-element.12.g_ref, bf16[256,768]{1,0:T(8,128)(2,1)S(1)} %bitcast.5, bf16[256,768]{1,0:T(8,128)(2,1)S(1)} %bitcast.6, s32[8,128]{1,0:T(8,128)S(1)} %get-tuple-element.15.tok_ref, ...), custom_call_target="tpu_custom_call" | custom-call | tf_op jit(solution)/shard_map/word_grad/pallas_call | solution.py:485
Async XLA Ops:
  0.6 0.9 %copy-start = (bf16[128,768]{1,0:T(8,128)(2,1)S(1)}, bf16[128,768]{1,0:T(8,128)(2,1)}, u32[]{:S(2)}) copy-start(bf16[128,768]{1,0:T(8,128)(2,1)} %hid_hbm.1) | copy-start | bytes 589828
  1.6 0.9 %copy-start.1 = (bf16[128,768]{1,0:T(8,128)(2,1)S(1)}, bf16[128,768]{1,0:T(8,128)(2,1)}, u32[]{:S(2)}) copy-start(bf16[128,768]{1,0:T(8,128)(2,1)} %emb_hbm.1) | copy-start | bytes 589828
  2.5 0.7 copy-start.2
  3.1 0.7 copy-start.3

commit v2 on v1

v2 whole, which is shorter than its diff:
```python
import functools

import jax
import jax.numpy as jnp
from jax import lax
from jax.experimental import pallas as pl
from jax.experimental.pallas import tpu as pltpu
from jax.sharding import PartitionSpec as P

MESH = pl.DeviceIdType.MESH
BF16, F32, I32, I16 = jnp.bfloat16, jnp.float32, jnp.int32, jnp.int16

DM = 768
VS = 6284
VH = 3142
SH = 6
MAIN = 3136
NC = 3200
CH = 640
NJ = NC // CH
ENDS = (0, 2, 4, NJ)
NP = len(ENDS) - 1
AHEAD = 2
NQ = NC + 128
LAG = 2
HN = 256
SR = 320
NS = 2 * NJ
TOP = 32767.0


class Place:
    def __init__(self):
        self.d = lax.axis_index("dp")
        self.p = lax.axis_index("pipe")
        self.t = lax.axis_index("tensor")
        self.c = self.p % 2
        self.k = self.p // 2

    def chip(self, k):
        return {"pipe": k * 2 + self.c}

    def partner(self):
        return {"pipe": self.k * 2 + (1 - self.c)}

    def group(self, g):
        return {"dp": g // 4, "tensor": g % 4}

    def row_group(self, g):
        return {"tensor": g // 2, "pipe": self.k * 2 + g % 2}

    def half_group(self, q):
        return {"dp": self.c, "pipe": q * 2 + self.d}


LN2_16 = 0.6931471805599453 / 16


def scale_of(code):
    return jnp.exp(code * LN2_16)


def quantize(x):
    top = jnp.maximum(jnp.max(jnp.abs(x), axis=-1, keepdims=True), 1e-30)
    code = jnp.ceil(jnp.log(top) * (1 / LN2_16) + 0.1)
    return jnp.round(x * (TOP / scale_of(code))).astype(I32).astype(I16), code


def comm_kernel(
    tok_ref, tgt_ref, hid_hbm, emb_hbm, w_hbm, tail_ref,
    g_out, hid_out, emb_out, tok_out, loss_out, hg_out,
    wwin, wsh, hid, emb, part, xch, qbuf, rs, tokx, lbuf, stat, gsend, gbuf,
    hgf, hq, hr,
    w_sem, hid_sem, px_send, px_recv, xc_send, xc_recv, rs_send, rs_recv,
    st_send, st_recv, ag_send, ag_recv, pf_send, pf_recv, hg_send, hg_recv,
    out_sem,
):
    me = Place()
    d, c, k = me.d, me.c, me.k
    h = c
    g_me = d * 4 + me.t
    r_me = me.t * 2 + h

    def remote(src, dst, ssem, rsem, to):
        return pltpu.make_async_remote_copy(
            src_ref=src, dst_ref=dst, send_sem=ssem, recv_sem=rsem, device_id=to, device_id_type=MESH
        )

    def w_copy(v, j):
        rows = CH if j < NJ - 1 else MAIN - (NJ - 1) * CH + (16 if v == 0 else 0)
        return pltpu.make_async_copy(
            w_hbm.at[pl.ds(v * MAIN + j * CH, rows)],
            wwin.at[v, pl.ds(j * CH, rows)],
            w_sem.at[v, j],
        )

    own_hid = pltpu.make_async_copy(hid_hbm, hid.at[d], hid_sem.at[0])
    own_hid.start()
    for j in range(AHEAD):
        for v in range(2):
            w_copy(v, j).start()
    own_emb = pltpu.make_async_copy(emb_hbm, emb.at[d], hid_sem.at[1])
    own_emb.start()

    bar = pltpu.get_barrier_semaphore()

    def greet(to):
        pl.semaphore_signal(bar, inc=1, device_id=to, device_id_type=MESH)

    greet(me.partner())
    for o in range(1, 8):
        greet(me.chip((k + o) % 8))
        greet(me.group((g_me + o) % 8))
    for o in range(1, 4):
        greet({"tensor": (me.t + o) % 4, "pipe": k * 2 + 1 - c})

    for q in range(8):
        greet({"dp": 1 - d, "pipe": q * 2 + 1 - c})
    pl.semaphore_wait(bar, 26)

    other = {"dp": 1 - d}
    give_hid = remote(hid.at[d], hid.at[d], px_send.at[0], px_recv.at[0], other)
    give_tok = remote(tok_ref, tokx, px_send.at[2], px_recv.at[2], other)
    give_tok.start()

    row16 = lax.broadcasted_iota(I32, (16, DM), 0)
    tail = jnp.where(row16 < VS - 2 * MAIN, tail_ref[...].astype(F32), 0.0)
    wwin[1, pl.ds(MAIN, 16), :] = tail.astype(BF16)
    for v in range(2):
        wwin[v, pl.ds(MAIN + 16, NC - MAIN), :] = jnp.zeros((NC - MAIN, DM), BF16)
    qbuf[:, :, pl.ds(NC, 128)] = jnp.zeros((8, 16, 128), I16)

    def xc_copy(s):
        return remote(part.at[s], xch.at[s // 2], xc_send.at[s // 2], xc_recv.at[s // 2], me.partner())

    def rs_copy(q, part_no, source):
        first, end = ENDS[part_no] * CH, ENDS[part_no + 1] * CH
        cols = pl.ds(first, (end if part_no < NP - 1 else NQ) - first)
        return remote(
            qbuf.at[q, :, cols], rs.at[source, :, cols], rs_send.at[part_no, q],
            rs_recv.at[part_no, source], me.chip(q),
        )

    def multiply(s):
        v = s % 2
        cols = pl.ds(pl.multiple_of((s // 2) * CH, CH), CH)
        prod = lax.dot_general(
            hid[d], wwin[v, cols, :], (((1,), (1,)), ((), ())), preferred_element_type=F32
        )
        part[s] = prod.reshape(8, 16, CH)

    def finish(j):
        xc_copy(2 * j + c).wait_recv()
        total = part[2 * j + c] + xch[j]
        code, scale = quantize(total)
        qbuf[:, :, pl.ds(pl.multiple_of(j * CH, CH), CH)] = code
        lane = lax.broadcasted_iota(I32, (8, 16, 128), 2)
        kept = qbuf[:, :, pl.ds(NC, 128)].astype(I32)
        kept = jnp.where(lane == j, scale.astype(I32), kept)
        qbuf[:, :, pl.ds(NC, 128)] = kept.astype(I16)
        for part_no in range(NP):

            @pl.when(j == ENDS[part_no + 1] - 1)
            def _():
                for o in range(1, 8):
                    rs_copy((k + o) % 8, part_no, k).start()

    own_hid.wait()
    give_hid.start()

    def step(j, carry):
        for jj in range(NJ):

            @pl.when(j == jj)
            def _():
                w_copy(0, jj).wait()
                w_copy(1, jj).wait()
                if jj + AHEAD < NJ:
                    w_copy(0, jj + AHEAD).start()
                    w_copy(1, jj + AHEAD).start()

        multiply(2 * j + 1 - c)
        xc_copy(2 * j + 1 - c).start()
        multiply(2 * j + c)

        @pl.when(j >= LAG)
        def _():
            finish(j - LAG)

        return carry

    lax.fori_loop(0, NJ, step, 0)

    def finish_step(j, carry):
        finish(j)
        return carry

    lax.fori_loop(NJ - LAG, NJ, finish_step, 0)
    rs[k] = qbuf[k]

    def shift(i, carry):
        rows = pl.multiple_of(i * SR, 64)
        wide = wwin[d, pl.ds(rows, SR + 16), :].astype(F32)
        moved = jnp.where(d == 0, wide[0:SR, :], wide[SH : SH + SR, :])
        wsh[pl.ds(rows, SR), :] = moved.astype(BF16)
        return carry

    lax.fori_loop(0, NC // SR, shift, 0)
    row_l = lax.broadcasted_iota(I32, (NC - MAIN, DM), 0) + MAIN
    end = wsh[pl.ds(MAIN, NC - MAIN), :].astype(F32)
    wsh[pl.ds(MAIN, NC - MAIN), :] = jnp.where(row_l < VH, end, 0.0).astype(BF16)

    lane16 = lax.broadcasted_iota(I32, (16, 128), 1)
    sub16 = lax.broadcasted_iota(I32, (16, 128), 0)
    tgt = jnp.sum(
        jnp.where(lane16 == sub16 + k * 16, tgt_ref[...].astype(F32), 0.0), axis=1, keepdims=True
    ).astype(I32)
    offset = me.t * VS + h * VH
    give_tok.wait_recv()
    sub8 = lax.broadcasted_iota(I32, (8, 128), 0)
    tok_out[...] = jnp.where(sub8 == d, tok_ref[...], tokx[...])

    for o in range(1, 8):
        for part_no in range(NP):
            rs_copy((k + o) % 8, part_no, (k + o) % 8).wait_recv()

    own_emb.wait()
    give_emb = remote(emb.at[d], emb.at[d], px_send.at[3], px_recv.at[3], other)
    give_emb.start()

    units = [scale_of(rs[q, :, NC:NQ].astype(I32).astype(F32)) * (1.0 / TOP) for q in range(8)]
    for j in range(NJ):
        total = jnp.zeros((16, CH), F32)
        for q in range(8):
            total += rs[q, :, j * CH : (j + 1) * CH].astype(I32).astype(F32) * units[q][:, j : j + 1]
        lbuf[:, j * CH : (j + 1) * CH] = total

    logits = pltpu.roll(lbuf[...], (NC - SH * h) % NC, 1)
    col = lax.broadcasted_iota(I32, (16, NC), 1)
    valid = col < VH
    logits = jnp.where(valid, logits, -1e30)
    chosen = jnp.logical_and(col == (tgt - offset), valid)
    m_loc = jnp.max(logits, axis=1, keepdims=True)
    e = jnp.where(valid, jnp.exp(logits - m_loc), 0.0)
    s_loc = jnp.sum(e, axis=1, keepdims=True)
    t_loc = jnp.sum(jnp.where(chosen, logits, 0.0), axis=1, keepdims=True)
    stat[r_me] = jnp.where(lane16 == 0, m_loc, jnp.where(lane16 == 1, s_loc, t_loc))

    def st_copy(o):
        return remote(
            stat.at[r_me], stat.at[r_me], st_send.at[o], st_recv.at[r_me], me.row_group((r_me + o) % 8)
        )

    for o in range(1, 8):
        st_copy(o).start()
    for o in range(1, 8):
        q = (r_me + o) % 8
        remote(stat.at[r_me], stat.at[q], st_send.at[o], st_recv.at[q], me.row_group(q)).wait_recv()
    row_max = stat[0][:, 0:1]
    for q in range(1, 8):
        row_max = jnp.maximum(row_max, stat[q][:, 0:1])
    row_total = jnp.zeros((16, 1), F32)
    target_logit = jnp.zeros((16, 1), F32)
    for q in range(8):
        row_total += stat[q][:, 1:2] * jnp.exp(stat[q][:, 0:1] - row_max)
        target_logit += stat[q][:, 2:3]
    loss = jnp.log(row_total) + row_max - target_logit
    grad = e * (jnp.exp(m_loc - row_max) / row_total) - jnp.where(chosen, 1.0, 0.0)
    hi = loss.astype(BF16).astype(F32)
    mid = (loss - hi).astype(BF16).astype(F32)
    low = loss - hi - mid
    grad = jnp.where(col == VH, hi, grad)
    grad = jnp.where(col == VH + 1, mid, grad)
    grad = jnp.where(col == VH + 2, low, grad)

    def rows_of(b):
        return pl.ds(pl.multiple_of(b * 16, 16), 16)

    gsend[...] = grad.astype(BF16)

    @pl.when(c == d)
    def _():
        gbuf[rows_of(d * 8 + k), :] = gsend[...]

    def ag_copy(q):
        return remote(
            gsend, gbuf.at[rows_of(d * 8 + k)], ag_send.at[q], ag_recv.at[k], me.half_group(q)
        )

    def pf_copy(u, core):
        rows = rows_of(core * 8 + u)
        return remote(gbuf.at[rows], gbuf.at[rows], pf_send.at[u], pf_recv.at[u], me.partner())

    def is_other(q):
        return jnp.logical_or(c != d, q != k)

    for o in range(8):
        q = (k + o) % 8

        @pl.when(is_other(q))
        def _():
            ag_copy(q).start()

    for o in range(8):
        u = (k + o) % 8

        @pl.when(is_other(u))
        def _():
            remote(
                gsend, gbuf.at[rows_of(c * 8 + u)], ag_send.at[0], ag_recv.at[u], me.partner()
            ).wait_recv()

        pf_copy(u, c).start()
    for u in range(8):
        pf_copy(u, 1 - c).wait_recv()

    g_copy = pltpu.make_async_copy(gbuf, g_out, out_sem.at[2])
    g_copy.start()
    give_hid.wait_recv()
    hid_copy = pltpu.make_async_copy(hid, hid_out, out_sem.at[1])
    hid_copy.start()
    give_emb.wait_recv()
    emb_copy = pltpu.make_async_copy(emb, emb_out, out_sem.at[0])
    emb_copy.start()

    def hg_copy(o):
        q = (g_me + o) % 8
        return remote(hq.at[q], hr.at[g_me], hg_send.at[o], hg_recv.at[g_me], me.group(q))

    def columns(n, carry):
        cols = pl.ds(pl.multiple_of(n * HN, HN), HN)
        hgf[:, cols] = jnp.dot(gbuf[...], wsh[:, cols], preferred_element_type=F32)
        return carry

    lax.fori_loop(0, DM // HN, columns, 0)
    code, scale = quantize(hgf[...].reshape(8, 32, DM))
    hq[:, :, 0:DM] = code
    hq[:, :, DM:] = jnp.broadcast_to(scale, (8, 32, 128)).astype(I32).astype(I16)
    for o in range(1, 8):
        hg_copy(o).start()
    hr[g_me] = hq[g_me]

    tile = gbuf[rows_of(d * 8 + me.p // 2), pl.ds(NC - 128, 128)].astype(F32)
    half = jnp.where(me.p % 2 == 0, tile[0:8, :], tile[8:16, :])
    lane8 = lax.broadcasted_iota(I32, (8, 128), 1)
    here = jnp.logical_and(lane8 >= VH - (NC - 128), lane8 < VH + 3 - (NC - 128))
    value = jnp.sum(jnp.where(here, half, 0.0), axis=1, keepdims=True)
    loss_out[...] = jnp.broadcast_to(value, (8, 128))

    for o in range(1, 8):
        q = (g_me + o) % 8
        remote(hq.at[q], hr.at[q], hg_send.at[o], hg_recv.at[q], me.group(q)).wait_recv()
    total = jnp.zeros((32, DM), F32)
    for q in range(8):
        unit = scale_of(hr[q, :, DM:].astype(I32).astype(F32))[:, 0:1] * (1.0 / TOP)
        total += hr[q, :, 0:DM].astype(I32).astype(F32) * unit
    hg_out[...] = total.astype(BF16)

    give_hid.wait_send()
    give_tok.wait_send()
    give_emb.wait_send()
    emb_copy.wait()
    hid_copy.wait()
    g_copy.wait()

    def drain(j, carry):
        xc_copy(2 * j + 1 - c).wait_send()
        return carry

    lax.fori_loop(0, NJ, drain, 0)
    for o in range(1, 8):
        for part_no in range(NP):
            rs_copy((k + o) % 8, part_no, k).wait_send()
    for o in range(1, 8):
        st_copy(o).wait_send()
    for q in range(8):

        @pl.when(is_other(q))
        def _():
            ag_copy(q).wait_send()

    for q in range(8):
        pf_copy(q, c).wait_send()
    for o in range(1, 8):
        hg_copy(o).wait_send()


def comm_call(tokens, targets, hidden, embed, word):
    any_, vmem = pl.BlockSpec(memory_space=pl.ANY), pl.BlockSpec(memory_space=pltpu.VMEM)
    dma = pltpu.SemaphoreType.DMA
    return pl.pallas_call(
        comm_kernel,
        grid=(1,),
        out_shape=(
            jax.ShapeDtypeStruct((256, NC), BF16),
            jax.ShapeDtypeStruct((2, 128, DM), BF16),
            jax.ShapeDtypeStruct((2, 128, DM), BF16),
            jax.ShapeDtypeStruct((8, 128), I32),
            jax.ShapeDtypeStruct((8, 128), F32),
            jax.ShapeDtypeStruct((32, DM), BF16),
        ),
        in_specs=[
            vmem, vmem, any_, any_, any_,
            pl.BlockSpec((16, DM), lambda i: (2 * MAIN // 16, 0)),
        ],
        out_specs=(any_, any_, any_, vmem, vmem, vmem),
        scratch_shapes=[
            pltpu.VMEM((2, NC + 16, DM), BF16),
            pltpu.VMEM((NC, DM), BF16),
            pltpu.VMEM((2, 128, DM), BF16),
            pltpu.VMEM((2, 128, DM), BF16),
            pltpu.VMEM((NS, 8, 16, CH), F32),
            pltpu.VMEM((NJ, 8, 16, CH), F32),
            pltpu.VMEM((8, 16, NQ), I16),
            pltpu.VMEM((8, 16, NQ), I16),
            pltpu.VMEM((1, 128), I32),
            pltpu.VMEM((16, NC), F32),
            pltpu.VMEM((8, 16, 128), F32),
            pltpu.VMEM((16, NC), BF16),
            pltpu.VMEM((256, NC), BF16),
            pltpu.VMEM((256, DM), F32),
            pltpu.VMEM((8, 32, DM + 128), I16),
            pltpu.VMEM((8, 32, DM + 128), I16),
            dma((2, NJ)),
            dma((2,)),
            dma((4,)),
            dma((4,)),
            dma((NJ,)),
            dma((NJ,)),
            dma((NP, 8)),
            dma((NP, 8)),
            dma((8,)),
            dma((8,)),
            dma((8,)),
            dma((8,)),
            dma((8,)),
            dma((8,)),
            dma((8,)),
            dma((8,)),
            dma((3,)),
        ],
        compiler_params=pltpu.CompilerParams(
            collective_id=0, has_side_effects=True, vmem_limit_bytes=60 * 2**20
        ),
        name="logit_grad",
    )(tokens, targets, hidden, embed, word, word)


RB = 640


def word_kernel(g_ref, hid_ref, emb_ref, tok_ref, loss_ref, hg_ref, out_ref, loss_out, hg_out):
    i = pl.program_id(0)
    base = lax.axis_index("tensor") * VS + lax.axis_index("dp") * VH + i * RB
    rows = lax.broadcasted_iota(I32, (RB, 128), 0) + base
    tok = tok_ref[...]
    hot = jnp.concatenate(
        [jnp.where(rows == tok[h : h + 1, :], 1.0, 0.0).astype(BF16) for h in range(2)], axis=1
    )
    head = lax.dot_general(
        g_ref[...], hid_ref[...], (((0,), (0,)), ((), ())), preferred_element_type=F32
    )
    out_ref[...] = head + jnp.dot(hot, emb_ref[...], preferred_element_type=F32)

    @pl.when(i == 0)
    def _():
        sub = lax.broadcasted_iota(I32, (8, 128), 0)
        lane = lax.broadcasted_iota(I32, (8, 128), 1)
        row = jnp.sum(jnp.where(sub == lane, loss_ref[...], 0.0), axis=0, keepdims=True)
        loss_out[...] = row[:, 0:8]
        hg_out[...] = hg_ref[...]


def word_call(grad, hid, emb, tok, loss, hg):
    def whole(*shape):
        return pl.BlockSpec(shape, lambda i: (0,) * len(shape))

    return pl.pallas_call(
        word_kernel,
        grid=(pl.cdiv(VH, RB),),
        out_shape=(
            jax.ShapeDtypeStruct((VH, DM), F32),
            jax.ShapeDtypeStruct((1, 8), F32),
            jax.ShapeDtypeStruct((32, DM), BF16),
        ),
        in_specs=[
            pl.BlockSpec((256, RB), lambda i: (0, i)),
            whole(256, DM), whole(256, DM), whole(8, 128), whole(8, 128), whole(32, DM),
        ],
        out_specs=(pl.BlockSpec((RB, DM), lambda i: (i, 0)), whole(1, 8), whole(32, DM)),
        compiler_params=pltpu.CompilerParams(vmem_limit_bytes=60 * 2**20),
        name="word_grad",
    )(grad, hid, emb, tok, loss, hg)


def local(tokens, targets, hidden, embed_grad, word_matrix):
    grad, hid, emb, tok, loss, hg = comm_call(
        tokens.reshape(1, 128), targets.reshape(1, 128), hidden, embed_grad, word_matrix
    )
    word, loss, hg = word_call(
        grad, hid.reshape(256, DM), emb.reshape(256, DM), tok, loss, hg
    )
    return loss.reshape(8), hg, word


def solution(mesh):
    return jax.shard_map(
        local,
        mesh=mesh,
        in_specs=(P("dp"), P("dp"), P("dp", "pipe"), P("dp", "pipe"), P("tensor", "pipe")),
        out_specs=(P(("dp", "pipe")), P(("dp", "tensor"), "pipe"), P(("tensor", "dp"), "pipe")),
        check_vma=False,
    )
```

time: 69.3 us -> 64.8 us (0.935)
  local copies, waits for them, and re-layouts: 3.16 us -> 0 us
  Pallas kernels: 65.3 us -> 63.9 us
    unnamed x8 -> x0, local copies, waits for them, and re-layouts: 3.16 us -> none
    pallas_call x1, Pallas kernels: 59.4 us -> 56.8 us  [comm_call(): pl.pallas_call(comm_kernel, grid=(1,), out_shape=(jax.ShapeDtypeStruct((2...]
    pallas_call x1, Pallas kernels: 5.95 us -> 7.08 us  [word_call(): pl.pallas_call(word_kernel, grid=(pl.cdiv(VH, RB),), out_shape=(jax.Shape...]
where the time goes in v2:
time: 64.8 us; the launch traced here: 64.5 us
  Pallas kernels  63.9 us (99%)
    pallas_call x1, Pallas kernels, comm_call(): pl.pallas_call(comm_kernel, grid=(1,), out_shape=(jax.ShapeDtypeStruct((2...  56.8 us
    pallas_call x1, Pallas kernels, word_call(): pl.pallas_call(word_kernel, grid=(pl.cdiv(VH, RB),), out_shape=(jax.Shape...  7.08 us

profile of v2, /device:TPU:1, one launch (start us, length us, event | category | flops | bytes accessed | tf_op | source)
XLA Modules:
  0.0 64.5 jit_solution(9076141293425347789)
XLA Ops:
  0.6 56.8 %logit_grad.1 = (bf16[256,3200]{1,0:T(8,128)(2,1)}, bf16[2,128,768]{2,1,0:T(8,128)(2,1)}, bf16[2,128,768]{2,1,0:T(8,128)(2,1)}, s32[8,128]{1,0:T(8,128)}, f32[8,128]{1,0:T(8,128)}, /*index=5*/bf16[32,768]{1,0:T(8,128)(2,1)}) custom-call(s32[1,128]{1,0:T(1,128)} %bitcast.7, s32[1,128]{1,0:T(1,128)} %bitcast.8, bf16[128,768]{1,0:T(8,128)(2,1)} %hid_hbm.1, ...), custom_call_target="tpu_custom_call" | custom-call | tf_op jit(solution)/shard_map/logit_grad/pallas_call | solution.py:391
  57.4 7.1 %word_grad.1 = (f32[3142,768]{1,0:T(8,128)}, f32[1,8]{1,0:T(1,128)}, bf16[32,768]{1,0:T(8,128)(2,1)}) custom-call(bf16[256,3200]{1,0:T(8,128)(2,1)} %get-tuple-element.12.g_ref, bf16[256,768]{1,0:T(8,128)(2,1)} %bitcast.5, bf16[256,768]{1,0:T(8,128)(2,1)} %bitcast.6, s32[8,128]{1,0:T(8,128)} %get-tuple-element.15.tok_ref, ...), custom_call_target="tpu_custom_call" | custom-call | tf_op jit(solution)/shard_map/word_grad/pallas_call | solution.py:478

commit v3 on v2

--- a/solution.py
+++ b/solution.py
@@ -302,7 +302,7 @@
             ag_copy(q).start()
 
     for o in range(8):
-        u = (k + o) % 8
+        u = (k + 8 - o) % 8
 
         @pl.when(is_other(u))
         def _():
@@ -446,7 +446,7 @@
     )(tokens, targets, hidden, embed, word, word)
 
 
-RB = 640
+RB = 1152
 
 
 def word_kernel(g_ref, hid_ref, emb_ref, tok_ref, loss_ref, hg_ref, out_ref, loss_out, hg_out):

time: 64.8 us -> 64.4 us (level)
  no operation moved by 1% of the time
where the time goes in v3:
time: 64.4 us; the launch traced here: 64.2 us
  Pallas kernels  63.5 us (99%)
    pallas_call x1, Pallas kernels, comm_call(): pl.pallas_call(comm_kernel, grid=(1,), out_shape=(jax.ShapeDtypeStruct((2...  56.8 us
    pallas_call x1, Pallas kernels, word_call(): pl.pallas_call(word_kernel, grid=(pl.cdiv(VH, RB),), out_shape=(jax.Shape...  6.79 us

profile of v3, /device:TPU:1, one launch (start us, length us, event | category | flops | bytes accessed | tf_op | source)
XLA Modules:
  0.0 64.2 jit_solution(13667032983584932922)
XLA Ops:
  0.6 56.8 %logit_grad.1 = (bf16[256,3200]{1,0:T(8,128)(2,1)}, bf16[2,128,768]{2,1,0:T(8,128)(2,1)}, bf16[2,128,768]{2,1,0:T(8,128)(2,1)}, s32[8,128]{1,0:T(8,128)}, f32[8,128]{1,0:T(8,128)}, /*index=5*/bf16[32,768]{1,0:T(8,128)(2,1)}) custom-call(s32[1,128]{1,0:T(1,128)} %bitcast.7, s32[1,128]{1,0:T(1,128)} %bitcast.8, bf16[128,768]{1,0:T(8,128)(2,1)} %hid_hbm.1, ...), custom_call_target="tpu_custom_call" | custom-call | tf_op jit(solution)/shard_map/logit_grad/pallas_call | solution.py:391
  57.4 6.8 %word_grad.1 = (f32[3142,768]{1,0:T(8,128)}, f32[1,8]{1,0:T(1,128)}, bf16[32,768]{1,0:T(8,128)(2,1)}) custom-call(bf16[256,3200]{1,0:T(8,128)(2,1)} %get-tuple-element.12.g_ref, bf16[256,768]{1,0:T(8,128)(2,1)} %bitcast.5, bf16[256,768]{1,0:T(8,128)(2,1)} %bitcast.6, s32[8,128]{1,0:T(8,128)} %get-tuple-element.15.tok_ref, ...), custom_call_target="tpu_custom_call" | custom-call | tf_op jit(solution)/shard_map/word_grad/pallas_call | solution.py:478

commit v4 on v3

--- a/solution.py
+++ b/solution.py
@@ -323,21 +323,31 @@
     emb_copy = pltpu.make_async_copy(emb, emb_out, out_sem.at[0])
     emb_copy.start()
 
-    def hg_copy(o):
-        q = (g_me + o) % 8
-        return remote(hq.at[q], hr.at[g_me], hg_send.at[o], hg_recv.at[g_me], me.group(q))
-
-    def columns(n, carry):
-        cols = pl.ds(pl.multiple_of(n * HN, HN), HN)
-        hgf[:, cols] = jnp.dot(gbuf[...], wsh[:, cols], preferred_element_type=F32)
-        return carry
-
-    lax.fori_loop(0, DM // HN, columns, 0)
-    code, scale = quantize(hgf[...].reshape(8, 32, DM))
-    hq[:, :, 0:DM] = code
-    hq[:, :, DM:] = jnp.broadcast_to(scale, (8, 32, 128)).astype(I32).astype(I16)
-    for o in range(1, 8):
-        hg_copy(o).start()
+    def hg_copy(q):
+        return remote(hq.at[q], hr.at[g_me], hg_send.at[q], hg_recv.at[g_me], me.group(q))
+
+    def hidden_rows(e):
+        rows = pl.ds(pl.multiple_of(e * 128, 128), 128)
+
+        def columns(n, carry):
+            cols = pl.ds(pl.multiple_of(n * HN, HN), HN)
+            hgf[:, cols] = jnp.dot(gbuf[rows, :], wsh[:, cols], preferred_element_type=F32)
+            return carry
+
+        lax.fori_loop(0, DM // HN, columns, 0)
+        code, scale = quantize(hgf[...].reshape(4, 32, DM))
+        four = pl.ds(e * 4, 4)
+        hq[four, :, 0:DM] = code
+        hq[four, :, DM:] = jnp.broadcast_to(scale, (4, 32, 128)).astype(I32).astype(I16)
+
+    far = [(1 - d) * 4 + (me.t + o) % 4 for o in range(4)]
+    near = [d * 4 + (me.t + o) % 4 for o in range(1, 4)]
+    hidden_rows(1 - d)
+    for q in far:
+        hg_copy(q).start()
+    hidden_rows(d)
+    for q in near:
+        hg_copy(q).start()
     hr[g_me] = hq[g_me]
 
     tile = gbuf[rows_of(d * 8 + me.p // 2), pl.ds(NC - 128, 128)].astype(F32)
@@ -347,9 +357,8 @@
     value = jnp.sum(jnp.where(here, half, 0.0), axis=1, keepdims=True)
     loss_out[...] = jnp.broadcast_to(value, (8, 128))
 
-    for o in range(1, 8):
-        q = (g_me + o) % 8
-        remote(hq.at[q], hr.at[q], hg_send.at[o], hg_recv.at[q], me.group(q)).wait_recv()
+    for q in far + near:
+        remote(hq.at[q], hr.at[q], hg_send.at[q], hg_recv.at[q], me.group(q)).wait_recv()
     total = jnp.zeros((32, DM), F32)
     for q in range(8):
         unit = scale_of(hr[q, :, DM:].astype(I32).astype(F32))[:, 0:1] * (1.0 / TOP)
@@ -381,8 +390,8 @@
 
     for q in range(8):
         pf_copy(q, c).wait_send()
-    for o in range(1, 8):
-        hg_copy(o).wait_send()
+    for q in far + near:
+        hg_copy(q).wait_send()
 
 
 def comm_call(tokens, targets, hidden, embed, word):
@@ -418,7 +427,7 @@
             pltpu.VMEM((8, 16, 128), F32),
             pltpu.VMEM((16, NC), BF16),
             pltpu.VMEM((256, NC), BF16),
-            pltpu.VMEM((256, DM), F32),
+            pltpu.VMEM((128, DM), F32),
             pltpu.VMEM((8, 32, DM + 128), I16),
             pltpu.VMEM((8, 32, DM + 128), I16),
             dma((2, NJ)),

time: 64.4 us -> 63.7 us (0.989)
    pallas_call x1, Pallas kernels: 56.8 us -> 56.1 us  [comm_call(): pl.pallas_call(comm_kernel, grid=(1,), out_shape=(jax.ShapeDtypeStruct((2...]
where the time goes in v4:
time: 63.7 us; the launch traced here: 63.5 us
  Pallas kernels  62.9 us (99%)
  between operations  0.64 us (1%)
    pallas_call x1, Pallas kernels, comm_call(): pl.pallas_call(comm_kernel, grid=(1,), out_shape=(jax.ShapeDtypeStruct((2...  56.1 us
    pallas_call x1, Pallas kernels, word_call(): pl.pallas_call(word_kernel, grid=(pl.cdiv(VH, RB),), out_shape=(jax.Shape...  6.79 us

profile of v4, /device:TPU:1, one launch (start us, length us, event | category | flops | bytes accessed | tf_op | source)
XLA Modules:
  0.0 63.5 jit_solution(14662668878552300106)
XLA Ops:
  0.6 56.1 %logit_grad.1 = (bf16[256,3200]{1,0:T(8,128)(2,1)}, bf16[2,128,768]{2,1,0:T(8,128)(2,1)}, bf16[2,128,768]{2,1,0:T(8,128)(2,1)}, s32[8,128]{1,0:T(8,128)}, f32[8,128]{1,0:T(8,128)}, /*index=5*/bf16[32,768]{1,0:T(8,128)(2,1)}) custom-call(s32[1,128]{1,0:T(1,128)} %bitcast.7, s32[1,128]{1,0:T(1,128)} %bitcast.8, bf16[128,768]{1,0:T(8,128)(2,1)} %hid_hbm.1, ...), custom_call_target="tpu_custom_call" | custom-call | tf_op jit(solution)/shard_map/logit_grad/pallas_call | solution.py:400
  56.7 6.8 %word_grad.1 = (f32[3142,768]{1,0:T(8,128)}, f32[1,8]{1,0:T(1,128)}, bf16[32,768]{1,0:T(8,128)(2,1)}) custom-call(bf16[256,3200]{1,0:T(8,128)(2,1)} %get-tuple-element.12.g_ref, bf16[256,768]{1,0:T(8,128)(2,1)} %bitcast.5, bf16[256,768]{1,0:T(8,128)(2,1)} %bitcast.6, s32[8,128]{1,0:T(8,128)} %get-tuple-element.15.tok_ref, ...), custom_call_target="tpu_custom_call" | custom-call | tf_op jit(solution)/shard_map/word_grad/pallas_call | solution.py:487
